TPU v7x, 32 devices: a whole 2x2x4 slice. The times are simulated.
32 devices in a mesh: mesh: 8 (over z, y), param: 4 (over x, core).
Axes of the slice: x: 2, y: 2, z: 4, core: 2. Of those that a mesh axis runs over, the one named last changes fastest.
Arguments:
- snapshots: bfloat16 [32768, 512], P('mesh', 'param'), may hold values from -4 to 4
- coupling: bfloat16 [256, 3, 128, 128], P('mesh'), may hold values from -0.3125 to 0.3125
- reaction_rate: float32 [512], P('param'), may hold values from 0.1 to 1
- sketch: bfloat16 [256, 128], replicated, may hold values from -0.375 to 0.375
Outputs:
- mode_basis: bfloat16 [32768, 128], P('mesh', 'param')
All inputs are finite; a program needn't handle non-finite values.
Results may differ from a plain program's by a relative error of at most 0.0095.
Values may be sent and summed in bfloat16 or wider, within the bound.
A program may use at most 64 MiB of HBM per device.

v0:
```python
import jax
import jax.numpy as jnp
from jax import lax
from jax.sharding import PartitionSpec as P

SECTIONS = 3


def extended_2(cells, sides, width):
    for axis, dim in sides:
        count = lax.axis_size(axis)
        ends = count - 1
        head = lax.slice_in_dim(cells, 0, width, axis=dim)
        tail = lax.slice_in_dim(cells, cells.shape[dim] - width, cells.shape[dim], axis=dim)
        cells = jnp.concatenate(
            [
                lax.ppermute(tail, axis, [(i, (i + 1) % count) for i in range(ends)]),
                cells,
                lax.ppermute(head, axis, [((i + 1) % count, i) for i in range(ends)]),
            ],
            axis=dim,
        )
    return cells


def from_partner(shard, axis, stride):
    return lax.ppermute(shard, axis, [(i, i ^ 1 << stride) for i in range(lax.axis_size(axis))])


def scaled_inverse(gram_matrix):
    cholesky_lower = jnp.linalg.cholesky(gram_matrix)
    identity_matrix = jnp.eye(gram_matrix.shape[0], dtype=gram_matrix.dtype)
    inverse = jax.scipy.linalg.solve_triangular(cholesky_lower, identity_matrix, lower=True)
    return inverse.T * jnp.diagonal(cholesky_lower)[None, :]


def column_gram(matrix, accurate):
    if accurate:
        return lax.dot_general(
            matrix, matrix, (((0,), (0,)), ((), ())), precision=lax.Precision.HIGHEST
        )
    return lax.dot_general(
        matrix, matrix, (((0,), (0,)), ((), ())), preferred_element_type=jnp.float32
    )


def on_device(snapshots, coupling, reaction_rate, sketch):
    state = snapshots
    unit_count, mode_count = state.shape
    block_size = coupling.shape[2]
    block_count = unit_count // block_size
    for section_index in range(SECTIONS):
        padded = extended_2(state, (("mesh", 0),), block_size)
        extended = padded.reshape(block_count + 2, block_size, mode_count)
        stacked = jnp.stack([extended[1:-1], extended[:-2], extended[2:]], 1)
        mixed_rows = jnp.einsum(
            "bkij,bkjm->bim", coupling, stacked, preferred_element_type=jnp.float32
        ).reshape(unit_count, mode_count)
        current = state.astype(jnp.float32)
        state = (
            (0.5 * current + 0.5 * mixed_rows) / (1.0 + reaction_rate[None, :] * current * current)
        ).astype(jnp.bfloat16)
    gram_matrix = lax.psum(column_gram(state, False), "mesh")
    leaf_factor = scaled_inverse(gram_matrix).astype(jnp.bfloat16)
    bases = jnp.dot(state, leaf_factor, preferred_element_type=jnp.float32).astype(jnp.bfloat16)
    param_count = lax.axis_size("param")
    tree_depth = param_count.bit_length() - 1
    position = lax.axis_index("param")
    for tree_level in range(tree_depth):
        upper_side = position // 2**tree_level % 2
        partner = from_partner(bases, "param", tree_level)
        lower_basis = jnp.where(upper_side == 0, bases, partner)
        upper_basis = jnp.where(upper_side == 0, partner, bases)
        joined = jnp.concatenate([lower_basis, upper_basis], 1)
        merged = jnp.dot(joined, sketch, preferred_element_type=jnp.float32)
        gram_matrix = lax.psum(column_gram(merged, True), "mesh")
        bases = jnp.dot(
            merged, scaled_inverse(gram_matrix), precision=lax.Precision.HIGHEST
        ).astype(jnp.bfloat16)
    column_share = mode_count // param_count
    return lax.dynamic_slice_in_dim(bases, position * column_share, column_share, 1)


def solution(mesh):
    return jax.shard_map(
        on_device,
        mesh=mesh,
        in_specs=(P("mesh", "param"), P("mesh", None, None, None), P("param"), P()),
        out_specs=P("mesh", "param"),
        check_vma=False,
    )
```

profile of v0, /device:TPU:0, one launch (start us, length us, event | category | flops | bytes accessed | tf_op | source)
XLA Modules:
  0.0 392.0 jit_solution(18107927483371434607)
XLA Ops:
  6.5 0.9 fusion.57
  7.5 5.0 %collective-permute-start = (bf16[128,128]{1,0:T(8,128)(2,1)S(1)}, bf16[128,128]{1,0:T(8,128)(2,1)S(1)}, u32[]{:S(2)}, u32[]{:S(2)}) collective-permute-start(bf16[128,128]{1,0:T(8,128)(2,1)S(1)} %get-tuple-element.27), channel_id=1, source_target_pairs={{0,4},{4,8},{8,12},{12,16},{16,20},{20,24},{24,28},{1,5},{5,9},{9,... | collective-permute-start | bytes 98312 | tf_op jit(solution)/shard_map/ppermute | solution.py:17
  12.5 1.3 collective-permute-start.1
  14.1 4.2 %collective-permute-done.1 = bf16[128,128]{1,0:T(8,128)(2,1)S(1)} collective-permute-done((bf16[128,128]{1,0:T(8,128)(2,1)S(1)}, bf16[128,128]{1,0:T(8,128)(2,1)S(1)}, u32[]{:S(2)}, u32[]{:S(2)}) %collective-permute-start.1) | collective-permute-done | bytes 32800 | tf_op jit(solution)/shard_map/ppermute | solution.py:19
  18.3 1.7 pad_maximum_fusion.5
  20.0 1.0 fusion
  21.0 0.6 fusion.20
  21.7 4.3 %collective-permute-start.2 = (bf16[128,128]{1,0:T(8,128)(2,1)S(1)}, bf16[128,128]{1,0:T(8,128)(2,1)S(1)}, u32[]{:S(2)}, u32[]{:S(2)}) collective-permute-start(bf16[128,128]{1,0:T(8,128)(2,1)S(1)} %get-tuple-element.23), channel_id=1, source_target_pairs={{0,4},{4,8},{8,12},{12,16},{16,20},{20,24},{24,28},{1,5},{5,9},{9,... | collective-permute-start | bytes 98312 | tf_op jit(solution)/shard_map/ppermute | solution.py:17
  26.0 1.3 collective-permute-start.3
  27.6 4.2 %collective-permute-done.3 = bf16[128,128]{1,0:T(8,128)(2,1)S(1)} collective-permute-done((bf16[128,128]{1,0:T(8,128)(2,1)S(1)}, bf16[128,128]{1,0:T(8,128)(2,1)S(1)}, u32[]{:S(2)}, u32[]{:S(2)}) %collective-permute-start.3) | collective-permute-done | bytes 32800 | tf_op jit(solution)/shard_map/ppermute | solution.py:19
  32.0 1.0 fusion.6
  33.0 0.6 fusion.23
  33.6 3.4 collective-permute-start.4
  37.1 1.3 collective-permute-start.5
  38.4 0.5 collective-permute-done.4
  38.9 4.0 %collective-permute-done.5 = bf16[128,128]{1,0:T(8,128)(2,1)S(1)} collective-permute-done((bf16[128,128]{1,0:T(8,128)(2,1)S(1)}, bf16[128,128]{1,0:T(8,128)(2,1)S(1)}, u32[]{:S(2)}, u32[]{:S(2)}) %collective-permute-start.5) | collective-permute-done | bytes 32800 | tf_op jit(solution)/shard_map/ppermute | solution.py:19
  43.0 1.0 fusion.12
  44.0 0.6 fusion.26
  44.7 1.0 copy-done.3
  45.6 1.1 fusion.58
  46.8 0.3 all-reduce.6.cloned.1.call-start
  47.1 68.5 %all-reduce.4.cloned.1.call-done = f32[128,128]{0,1:T(8,128)} async-done(((f32[128,128]{0,1:T(8,128)}), f32[128,128]{0,1:T(8,128)}) %all-reduce.4.cloned.1.call-update) | async-done | bytes 65552 | tf_op jit(solution)/shard_map/psum | solution.py:63
  115.6 0.9 copy.12
  116.5 0.9 fusion.47
  117.4 11.7 %cholesky.59 = f32[128,128]{1,0:T(8,128)S(1)} custom-call(f32[128,128]{1,0:T(8,128)S(1)} %fusion.47), custom_call_target="Cholesky" | custom-call | tf_op jit(solution)/shard_map/jit(cholesky)/cholesky | solution.py:31
  129.1 0.6 compare_reduce_fusion.2
  129.7 0.7 select_bitcast_fusion.2
  130.4 9.8 %custom-call.13 = f32[1,128,128]{1,2,0:T(8,128)S(1)} custom-call(f32[1,128,128]{2,1,0:T(8,128)S(1)} %get-tuple-element.11), custom_call_target="InvertDiagBlocksLowerTriangular" | custom-call | tf_op jit(solution)/shard_map/jit(_solve_triangular)/triangular_solve | solution.py:33
  140.2 1.2 gather_fusion
  141.5 0.3 fusion.38
  141.8 2.7 convolution_convert_fusion.1
  144.5 3.0 collective-permute-done.6
  147.5 1.7 broadcast_select_fusion.1
  149.2 0.8 fusion.30
  149.9 1.3 copy-done.2
  151.3 4.1 %fusion.59 = f32[128,128]{0,1:T(8,128)} fusion(f32[4096,128]{1,0:T(8,128)S(1)} %fusion.30), kind=kOutput, calls=%fused_computation.100 | convolution fusion | flops 805306368 | bytes 2162688 | tf_op jit(solution)/shard_map/dot_general | solution.py:39
  155.4 12.9 %all-reduce.8.cloned.1.call-start = ((), (), s32[]{:S(2)}) async-start(), calls=%async_computation.2 | async-start | bytes 131072 | tf_op jit(solution)/shard_map/psum | solution.py:76
  168.2 55.7 %all-reduce.6.cloned.1.call-done = f32[128,128]{0,1:T(8,128)} async-done(((f32[128,128]{0,1:T(8,128)}), f32[128,128]{0,1:T(8,128)}) %all-reduce.6.cloned.1.call-update) | async-done | bytes 65552 | tf_op jit(solution)/shard_map/psum | solution.py:76
  224.0 0.9 copy.14
  224.9 0.9 fusion.45
  225.8 11.7 %cholesky.70 = f32[128,128]{1,0:T(8,128)S(1)} custom-call(f32[128,128]{1,0:T(8,128)S(1)} %fusion.45), custom_call_target="Cholesky" | custom-call | tf_op jit(solution)/shard_map/jit(cholesky)/cholesky | solution.py:31
  237.5 0.6 compare_reduce_fusion.1
  238.2 0.7 select_bitcast_fusion.1
  238.8 9.8 %custom-call.14 = f32[1,128,128]{1,2,0:T(8,128)S(1)} custom-call(f32[1,128,128]{2,1,0:T(8,128)S(1)} %get-tuple-element.9), custom_call_target="InvertDiagBlocksLowerTriangular" | custom-call | tf_op jit(solution)/shard_map/jit(_solve_triangular)/triangular_solve | solution.py:33
  248.6 1.2 gather_fusion.1
  249.9 0.3 convolution_multiply_fusion.1
  250.2 4.5 %convolution_convert_fusion = bf16[4096,128]{0,1:T(8,128)(2,1)} fusion(f32[4096,128]{1,0:T(8,128)} %copy-done.2, f32[128,128]{1,0:T(8,128)S(1)} %convolution_multiply_fusion.1), kind=kOutput, calls=%fused_computation.3 | convolution fusion | flops 805830656 | bytes 3211264 | tf_op jit(solution)/shard_map/dot_general | solution.py:77
  254.7 1.5 collective-permute-start.7
  256.2 21.9 %collective-permute-done.7 = bf16[4096,128]{0,1:T(8,128)(2,1)} collective-permute-done((bf16[4096,128]{0,1:T(8,128)(2,1)}, bf16[4096,128]{0,1:T(8,128)(2,1)}, u32[]{:S(2)}, u32[]{:S(2)}) %collective-permute-start.7) | collective-permute-done | bytes 1048608 | tf_op jit(solution)/shard_map/ppermute | solution.py:27
  278.1 1.7 broadcast_select_fusion.3
  279.8 0.8 fusion.34
  280.6 1.3 copy-done.1
  281.9 4.1 %fusion.60 = f32[128,128]{0,1:T(8,128)} fusion(f32[4096,128]{1,0:T(8,128)S(1)} %fusion.34), kind=kOutput, calls=%fused_computation.101 | convolution fusion | flops 805306368 | bytes 2162688 | tf_op jit(solution)/shard_map/dot_general | solution.py:39
  286.0 68.5 %all-reduce.8.cloned.1.call-done = f32[128,128]{0,1:T(8,128)} async-done(((f32[128,128]{0,1:T(8,128)}), f32[128,128]{0,1:T(8,128)}) %all-reduce.8.cloned.1.call-update) | async-done | bytes 65552 | tf_op jit(solution)/shard_map/psum | solution.py:76
  354.5 0.9 copy.16
  355.5 0.9 fusion.43
  356.3 11.7 %cholesky.81 = f32[128,128]{1,0:T(8,128)S(1)} custom-call(f32[128,128]{1,0:T(8,128)S(1)} %fusion.43), custom_call_target="Cholesky" | custom-call | tf_op jit(solution)/shard_map/jit(cholesky)/cholesky | solution.py:31
  368.1 0.6 compare_reduce_fusion
  368.7 0.7 select_bitcast_fusion
  369.4 10.0 %custom-call.15 = f32[1,128,128]{1,2,0:T(8,128)S(1)} custom-call(f32[1,128,128]{2,1,0:T(8,128)S(1)} %get-tuple-element.6), custom_call_target="InvertDiagBlocksLowerTriangular" | custom-call | tf_op jit(solution)/shard_map/jit(_solve_triangular)/triangular_solve | solution.py:33
  379.4 1.2 gather_fusion.2
  380.6 0.3 convolution_multiply_fusion
  380.9 3.6 fusion.61
  384.5 0.7 dynamic-slice_convert_fusion
  (26 shorter events, 1.0 us)
Async XLA Ops:
  6.5 13.4 %copy-start = (bf16[32,3,128,128]{3,2,1,0:T(8,128)(2,1)S(1)}, bf16[32,3,128,128]{3,2,1,0:T(8,128)(2,1)}, u32[]{:S(2)}) copy-start(bf16[32,3,128,128]{3,2,1,0:T(8,128)(2,1)} %param.8) | copy-start | bytes 9437188
  6.5 109.0 %all-reduce.4.cloned.1.call-start = ((), (), s32[]{:S(2)}) async-start(), calls=%async_computation | async-start | bytes 131072 | tf_op jit(solution)/shard_map/psum | solution.py:63
  6.5 13.4 %copy-start.4 = (bf16[4096,128]{1,0:T(8,128)(2,1)S(1)}, bf16[4096,128]{1,0:T(8,128)(2,1)}, u32[]{:S(2)}) copy-start(bf16[4096,128]{1,0:T(8,128)(2,1)} %param.7) | copy-start | bytes 3145732
  7.5 6.6 %collective-permute-start = (bf16[128,128]{1,0:T(8,128)(2,1)S(1)}, bf16[128,128]{1,0:T(8,128)(2,1)S(1)}, u32[]{:S(2)}, u32[]{:S(2)}) collective-permute-start(bf16[128,128]{1,0:T(8,128)(2,1)S(1)} %get-tuple-element.27), channel_id=1, source_target_pairs={{0,4},{4,8},{8,12},{12,16},{16,20},{20,24},{24,28},{1,5},{5,9},{9,... | collective-permute-start | bytes 98312 | tf_op jit(solution)/shard_map/ppermute | solution.py:17
  12.5 5.8 %collective-permute-start.1 = (bf16[128,128]{1,0:T(8,128)(2,1)S(1)}, bf16[128,128]{1,0:T(8,128)(2,1)S(1)}, u32[]{:S(2)}, u32[]{:S(2)}) collective-permute-start(bf16[128,128]{1,0:T(8,128)(2,1)S(1)} %get-tuple-element.28), channel_id=1, source_target_pairs={{4,0},{8,4},{12,8},{16,12},{20,16},{24,20},{28,24},{5,1},{9,5},{13... | collective-permute-start | bytes 98312 | tf_op jit(solution)/shard_map/ppermute | solution.py:19
  20.0 1.0 copy-start.6
  21.7 5.9 %collective-permute-start.2 = (bf16[128,128]{1,0:T(8,128)(2,1)S(1)}, bf16[128,128]{1,0:T(8,128)(2,1)S(1)}, u32[]{:S(2)}, u32[]{:S(2)}) collective-permute-start(bf16[128,128]{1,0:T(8,128)(2,1)S(1)} %get-tuple-element.23), channel_id=1, source_target_pairs={{0,4},{4,8},{8,12},{12,16},{16,20},{20,24},{24,28},{1,5},{5,9},{9,... | collective-permute-start | bytes 98312 | tf_op jit(solution)/shard_map/ppermute | solution.py:17
  26.0 5.8 %collective-permute-start.3 = (bf16[128,128]{1,0:T(8,128)(2,1)S(1)}, bf16[128,128]{1,0:T(8,128)(2,1)S(1)}, u32[]{:S(2)}, u32[]{:S(2)}) collective-permute-start(bf16[128,128]{1,0:T(8,128)(2,1)S(1)} %get-tuple-element.24), channel_id=1, source_target_pairs={{4,0},{8,4},{12,8},{16,12},{20,16},{24,20},{28,24},{5,1},{9,5},{13... | collective-permute-start | bytes 98312 | tf_op jit(solution)/shard_map/ppermute | solution.py:19
  33.6 5.2 %collective-permute-start.4 = (bf16[128,128]{1,0:T(8,128)(2,1)S(1)}, bf16[128,128]{1,0:T(8,128)(2,1)S(1)}, u32[]{:S(2)}, u32[]{:S(2)}) collective-permute-start(bf16[128,128]{1,0:T(8,128)(2,1)S(1)} %get-tuple-element.19), channel_id=1, source_target_pairs={{0,4},{4,8},{8,12},{12,16},{16,20},{20,24},{24,28},{1,5},{5,9},{9,... | collective-permute-start | bytes 98312 | tf_op jit(solution)/shard_map/ppermute | solution.py:17
  37.1 5.8 %collective-permute-start.5 = (bf16[128,128]{1,0:T(8,128)(2,1)S(1)}, bf16[128,128]{1,0:T(8,128)(2,1)S(1)}, u32[]{:S(2)}, u32[]{:S(2)}) collective-permute-start(bf16[128,128]{1,0:T(8,128)(2,1)S(1)} %get-tuple-element.20), channel_id=1, source_target_pairs={{4,0},{8,4},{12,8},{16,12},{20,16},{24,20},{28,24},{5,1},{9,5},{13... | collective-permute-start | bytes 98312 | tf_op jit(solution)/shard_map/ppermute | solution.py:19
  44.7 1.0 copy-start.3
  46.8 177.2 %all-reduce.6.cloned.1.call-start = ((), (), s32[]{:S(2)}) async-start(), calls=%async_computation.1 | async-start | bytes 131072 | tf_op jit(solution)/shard_map/psum | solution.py:76
  144.5 3.0 collective-permute-start.6
  144.5 4.7 %copy-start.5 = (bf16[256,128]{1,0:T(8,128)(2,1)S(1)}, bf16[256,128]{1,0:T(8,128)(2,1)}, u32[]{:S(2)}) copy-start(bf16[256,128]{1,0:T(8,128)(2,1)} %param.10) | copy-start | bytes 196612
  149.9 1.3 copy-start.2
  155.4 199.2 %all-reduce.8.cloned.1.call-start = ((), (), s32[]{:S(2)}) async-start(), calls=%async_computation.2 | async-start | bytes 131072 | tf_op jit(solution)/shard_map/psum | solution.py:76
  254.7 23.4 %collective-permute-start.7 = (bf16[4096,128]{0,1:T(8,128)(2,1)}, bf16[4096,128]{0,1:T(8,128)(2,1)}, u32[]{:S(2)}, u32[]{:S(2)}) collective-permute-start(bf16[4096,128]{0,1:T(8,128)(2,1)} %convolution_convert_fusion), channel_id=1, source_target_pairs={{0,2},{1,3},{2,0},{3,1},{4,6},{5,7},{6,4},{7,5},{8,10},{9,11},{10,... | collective-permute-start | bytes 3145736 | tf_op jit(solution)/shard_map/ppermute | solution.py:27
  280.6 1.3 copy-start.1
Sparse Core Ops, SparseCore 0:
  46.9 68.6 all-reduce.3
  155.5 68.4 all-reduce.5
  286.1 68.3 all-reduce.7
where the time goes:
time: 398 us; the launch traced here: 392 us
  waiting for transfers between devices  231 us (58%)
  other arithmetic  78.5 us (20%)
  starting transfers between devices  31.3 us (8%)
  matrix products  25.5 us (6%)
  between operations  13.7 us (3%)
  local copies, waits for them, and re-layouts  11.8 us (3%)
    psum x2, waiting for transfers between devices, on_device(): gram_matrix = lax.psum(column_gram(merged, True), 'mesh')  124 us
    psum x1, waiting for transfers between devices, on_device(): gram_matrix = lax.psum(column_gram(state, False), 'mesh')  68.5 us
    another operation x9, other arithmetic, scaled_inverse(): cholesky_lower = jnp.linalg.cholesky(gram_matrix)  37.2 us
    another operation x6, other arithmetic, scaled_inverse(): jax.scipy.linalg.solve_triangular(cholesky_lower, identity_matrix, lower=...  31.6 us
    ppermute x2, waiting for transfers between devices, from_partner(): lax.ppermute(shard, axis, [(i, i ^ 1 << stride) for i in range(lax.axis_s...  24.9 us
    psum x2, starting transfers between devices, on_device(): gram_matrix = lax.psum(column_gram(merged, True), 'mesh')  13.2 us
    ppermute x3, starting transfers between devices, extended_2(): lax.ppermute(tail, axis, [(i, (i + 1) % count) for i in range(ends)])  12.7 us
    ppermute x3, waiting for transfers between devices, extended_2(): lax.ppermute(head, axis, [((i + 1) % count, i) for i in range(ends)])  12.5 us
  transfers between devices with their start and end apart: 11, of which 11 were waited for; matrix products, arithmetic and copies ran while one was open for 0% of the time, Pallas kernels for 0%

commit v1 on v0

v1 whole, which is shorter than its diff:
```python
import functools

import jax
import jax.numpy as jnp
from jax import lax
from jax.experimental import pallas as pl
from jax.experimental.pallas import tpu as pltpu
from jax.sharding import PartitionSpec as P

SECTIONS = 3
MESH = pl.DeviceIdType.MESH
F32 = jnp.float32
BF16 = jnp.bfloat16


def split_two(x):
    high = x.astype(BF16)
    return high, (x - high.astype(F32)).astype(BF16)


def unit_inverse(gram):
    size = gram.shape[0]
    count = size // 8
    rows = [gram[8 * q : 8 * q + 8, :] for q in range(count)]
    lane = lax.broadcasted_iota(jnp.int32, (8, size), 1)
    sub = lax.broadcasted_iota(jnp.int32, (8, size), 0)
    for p in range(count):
        first = 8 * p
        inside = (lane >= first) & (lane < first + 8)
        columns = [
            [jnp.broadcast_to(rows[q][:, first + j : first + j + 1], (8, size)) for j in range(8)]
            for q in range(p, count)
        ]
        work = [jnp.where(inside, jnp.where(lane - first == sub, 1.0, 0.0), rows[p])]
        work += [jnp.where(inside, 0.0, rows[q]) for q in range(p + 1, count)]
        for i in range(8):
            pivot_row = jnp.broadcast_to(work[0][i : i + 1, :], (8, size))
            entries = [jnp.broadcast_to(columns[0][j][i : i + 1, :], (8, size)) for j in range(i, 8)]
            inverse = 1.0 / entries[0]
            for q in range(count - p):
                scale = columns[q][i] * inverse
                if q == 0:
                    scale = jnp.where(sub > i, scale, 0.0)
                work[q] = work[q] - scale * pivot_row
                for j in range(i + 1, 8):
                    columns[q][j] = columns[q][j] - scale * entries[j - i]
        rows[p:] = work
    full = jnp.concatenate(rows, 0)
    row = lax.broadcasted_iota(jnp.int32, (size, size), 0)
    column = lax.broadcasted_iota(jnp.int32, (size, size), 1)
    return jnp.where(column <= row, full, 0.0)


def cross(a, b):
    return lax.dot_general(a, b, (((0,), (0,)), ((), ())), preferred_element_type=F32)


def dot(a, b):
    return jnp.dot(a, b, preferred_element_type=F32)


def wait_bytes(ref, sem):
    pltpu.make_async_copy(ref, ref, sem).wait()


def kernel(plan, snap_ref, coup_ref, rate_ref, sketch_ref, out_ref, *scratch):
    n_mesh, n_param, levels, pieces = plan
    scratch = list(scratch)
    take = lambda k: [scratch.pop(0) for _ in range(k)]
    coup, packed, landed, tall = take(4)
    states = take(SECTIONS + 1)
    bases = take(levels)
    partner_rows = take(levels)
    halves = take(levels)
    partial = take(levels + 1)
    slots = take(levels + 1)
    grams = take(levels + 1)
    load_sem, halo_send, halo_recv, merge_send, merge_recv, sum_send, sum_recv, all_send, all_recv, out_send, out_recv = take(11)

    m = lax.axis_index("mesh")
    p = lax.axis_index("param")
    total_rows, modes = snap_ref.shape
    block_count, _, block, _ = coup_ref.shape

    load_state = pltpu.make_async_copy(snap_ref, states[0].at[pl.ds(block, total_rows)], load_sem.at[0])
    load_coup = pltpu.make_async_copy(coup_ref, coup, load_sem.at[1])
    load_state.start()
    load_coup.start()

    n_all = n_mesh * n_param
    me = m * n_param + p
    barrier = pltpu.get_barrier_semaphore()

    def greet(s, carry):
        t = lax.rem(me + s, n_all)
        pl.semaphore_signal(barrier, inc=1, device_id=(t // n_param, lax.rem(t, n_param)), device_id_type=MESH)
        return carry

    lax.fori_loop(1, n_all, greet, 0)
    for k in range(SECTIONS):
        @pl.when(m == 0)
        def _():
            states[k][pl.ds(0, block), :] = jnp.zeros((block, modes), BF16)

        @pl.when(m == n_mesh - 1)
        def _():
            states[k][pl.ds(block + total_rows, block), :] = jnp.zeros((block, modes), BF16)
    load_state.wait()
    pl.semaphore_wait(barrier, n_all - 1)

    def halo_up(k):
        return pltpu.make_async_remote_copy(
            states[k].at[pl.ds(total_rows, block)], states[k].at[pl.ds(0, block)],
            halo_send.at[2 * k], halo_recv.at[2 * k], device_id=(m + 1, p), device_id_type=MESH)

    def halo_down(k):
        return pltpu.make_async_remote_copy(
            states[k].at[pl.ds(block, block)], states[k].at[pl.ds(block + total_rows, block)],
            halo_send.at[2 * k + 1], halo_recv.at[2 * k + 1], device_id=(m - 1, p), device_id_type=MESH)

    def halo_start(k):
        @pl.when(m < n_mesh - 1)
        def _():
            halo_up(k).start()

        @pl.when(m > 0)
        def _():
            halo_down(k).start()

    halo_start(0)
    load_coup.wait()
    rate = rate_ref[...]

    def advance(k, b):
        c = coup.at[b]
        operator = jnp.concatenate([c[1], c[0], c[2]], 1)
        start = pl.multiple_of(b * block, block)
        mixed = dot(operator, states[k][pl.ds(start, 3 * block), :])
        at = pl.ds(pl.multiple_of(start + block, block), block)
        current = states[k][at, :].astype(F32)
        states[k + 1][at, :] = ((0.5 * current + 0.5 * mixed) / (1.0 + rate * current * current)).astype(BF16)

    inner = block_count - 2
    group = max(g for g in range(1, 11) if inner % g == 0)
    for k in range(SECTIONS):
        def some(i, carry, k=k):
            for j in range(group):
                advance(k, 1 + i * group + j)
            return carry

        lax.fori_loop(0, inner // group, some, 0)

        @pl.when(m > 0)
        def _():
            halo_up(k).wait_recv()

        @pl.when(m < n_mesh - 1)
        def _():
            halo_down(k).wait_recv()

        advance(k, 0)
        advance(k, block_count - 1)
        if k + 1 < SECTIONS:
            halo_start(k + 1)
    state = states[SECTIONS]

    def sum_over(level):
        width = 2**level
        n = n_mesh * width
        count = min(n, pieces)
        depth = modes // count
        base = p // width * width
        rank = m * width + (p - base)

        def device(t):
            return (t // width, base + lax.rem(t, width))

        def scatter(s, carry):
            t = lax.rem(rank + s, n)
            at = pl.ds(pl.multiple_of(lax.rem(t, count) * depth, depth), depth)
            pltpu.make_async_remote_copy(
                partial[level].at[at], slots[level].at[s - 1], sum_send.at[level], sum_recv.at[level],
                device_id=device(t), device_id_type=MESH).start()
            return carry

        lax.fori_loop(1, n, scatter, 0)
        piece = lax.rem(rank, count)
        own = pl.ds(pl.multiple_of(piece * depth, depth), depth)
        wait_bytes(slots[level], sum_recv.at[level])
        if n <= 64:
            total = partial[level][own, :] + jnp.sum(slots[level][...], 0)
        else:
            total = partial[level][own, :] + lax.fori_loop(
                0, n - 1, lambda i, a: a + slots[level][i], jnp.zeros((depth, modes), F32))
        grams[level][own, :] = total

        def spread(s, carry):
            t = rank - piece + lax.rem(piece + s, count)
            pltpu.make_async_remote_copy(
                grams[level].at[own], grams[level].at[own], all_send.at[level], all_recv.at[level],
                device_id=device(t), device_id_type=MESH).start()
            return carry

        lax.fori_loop(1, count, spread, 0)
        wait_bytes(grams[level].at[pl.ds(0, (count - 1) * depth)], all_recv.at[level])
        return grams[level][...]

    chunk = 512
    gram = jnp.zeros((modes, modes), F32)
    for i in range(total_rows // chunk):
        part = state[pl.ds(block + i * chunk, chunk), :]
        gram += cross(part, part)
    partial[0][...] = gram
    factor = unit_inverse(sum_over(0)).T.astype(BF16)

    def merge_copy(level):
        held = total_rows // 2**level
        keep = p // 2**level % 2
        away = pl.ds(pl.multiple_of((1 - keep) * (held // 2), 16), held // 2)
        return pltpu.make_async_remote_copy(
            bases[level].at[away], partner_rows[level], merge_send.at[level], merge_recv.at[level],
            device_id=(m, p + (1 - 2 * keep) * 2**level), device_id_type=MESH)

    for level in range(levels):
        held = total_rows // 2**level
        half = held // 2
        keep = p // 2**level % 2
        step = min(half, chunk)
        for side in range(2):
            first = (1 - keep if side == 0 else keep) * half
            for i in range(half // step):
                at = pl.multiple_of(first + i * step, 16)
                if level == 0:
                    basis = dot(state[pl.ds(pl.multiple_of(at + block, 16), step), :], factor)
                else:
                    pair = halves[level - 1][pl.ds(at, step), :]
                    basis = dot(pair, twice) + dot(pair[:, :modes], rest)
                bases[level][pl.ds(at, step), :] = basis.astype(BF16)
            if side == 0:
                merge_copy(level).start()
        mine = sketch_ref[pl.ds(pl.multiple_of(keep * modes, modes), modes), :]
        theirs = sketch_ref[pl.ds(pl.multiple_of((1 - keep) * modes, modes), modes), :]
        weights = jnp.concatenate([mine, theirs], 0)
        merge_copy(level).wait_recv()
        gram = jnp.zeros((modes, 2 * modes), F32)
        for i in range(half // step):
            own = bases[level][pl.ds(pl.multiple_of(keep * half + i * step, 16), step), :]
            other = partner_rows[level][pl.ds(i * step, step), :]
            high, low = split_two(dot(jnp.concatenate([own, other], 1), weights))
            pair = jnp.concatenate([high, low], 1)
            halves[level][pl.ds(i * step, step), :] = pair
            gram += cross(high, pair)
        partial[level + 1][...] = gram[:, :modes] + gram[:, modes:] + gram[:, modes:].T
        high, rest = split_two(unit_inverse(sum_over(level + 1)).T)
        twice = jnp.concatenate([high, high], 0)

    share = modes // n_param
    rows = total_rows // n_param
    cut = rows // n_param
    for i in range(n_param):
        pair = halves[levels - 1][pl.ds(i * cut, cut), :]
        tall[pl.ds(i * cut, cut), :] = dot(pair, twice) + dot(pair[:, :modes], rest)
    lane = lax.broadcasted_iota(jnp.int32, (cut, modes), 1) // share
    for q in range(n_param):
        value = jnp.zeros((cut, modes), F32)
        for a in range(n_param):
            turned = tall[pl.ds(a * cut, cut), :]
            if a != q:
                turned = pltpu.roll(turned, (a - q) % n_param * share, 1)
            value = jnp.where(lane == a, turned, value)
        packed[q] = value.astype(BF16)

    def deliver(s, carry):
        t = lax.rem(p + s, n_param)
        pltpu.make_async_remote_copy(
            packed.at[t], landed.at[s - 1], out_send.at[0], out_recv.at[0],
            device_id=(m, t), device_id_type=MESH).start()
        return carry

    lax.fori_loop(1, n_param, deliver, 0)

    def unpack(source, value):
        start = 0
        for level in range(levels):
            start = start + source // 2**level % 2 * (total_rows // 2 ** (level + 1))
        for a in range(n_param):
            turned = value if a == 0 else pltpu.roll(value, (n_param - a) * share, 1)
            out_ref[pl.ds(pl.multiple_of(start + a * cut, 16), cut), :] = turned[:, :share].astype(BF16)

    unpack(p, packed[p].astype(F32))
    wait_bytes(landed, out_recv.at[0])
    for s in range(1, n_param):
        unpack(lax.rem(p + n_param - s, n_param), landed[s - 1].astype(F32))

    for k in range(SECTIONS):
        @pl.when(m < n_mesh - 1)
        def _():
            halo_up(k).wait_send()

        @pl.when(m > 0)
        def _():
            halo_down(k).wait_send()
    for level in range(levels):
        merge_copy(level).wait_send()
    for level in range(levels + 1):
        count = min(n_mesh * 2**level, pieces)
        wait_bytes(slots[level], sum_send.at[level])
        wait_bytes(grams[level].at[pl.ds(0, (count - 1) * (modes // count))], all_send.at[level])
    wait_bytes(landed, out_send.at[0])


def solution(mesh):
    n_mesh, n_param = mesh.shape["mesh"], mesh.shape["param"]
    levels = n_param.bit_length() - 1

    def on_device(snapshots, coupling, reaction_rate, sketch):
        rows, modes = snapshots.shape
        block = coupling.shape[2]
        pieces = modes // 8
        square = pltpu.VMEM((modes, modes), F32)
        slots = []
        for level in range(levels + 1):
            n = n_mesh * 2**level
            slots.append(pltpu.VMEM((n - 1, modes // min(n, pieces), modes), F32))
        cut = rows // n_param // n_param
        dma = lambda k: pltpu.SemaphoreType.DMA((k,))
        scratch = [
            pltpu.VMEM(coupling.shape, BF16),
            pltpu.VMEM((n_param, cut, modes), BF16),
            pltpu.VMEM((n_param - 1, cut, modes), BF16),
            pltpu.VMEM((rows // n_param, modes), F32),
        ]
        scratch += [pltpu.VMEM((rows + 2 * block, modes), BF16)] * (SECTIONS + 1)
        scratch += [pltpu.VMEM((rows >> k, modes), BF16) for k in range(levels)]
        scratch += [pltpu.VMEM((rows >> (k + 1), modes), BF16) for k in range(levels)]
        scratch += [pltpu.VMEM((rows >> (k + 1), 2 * modes), BF16) for k in range(levels)]
        scratch += [square] * (levels + 1) + slots + [square] * (levels + 1)
        scratch += [dma(2), dma(2 * SECTIONS), dma(2 * SECTIONS), dma(levels), dma(levels)]
        scratch += [dma(levels + 1)] * 4 + [dma(1), dma(1)]
        vmem = pl.BlockSpec(memory_space=pltpu.VMEM)
        anywhere = pl.BlockSpec(memory_space=pl.ANY)
        return pl.pallas_call(
            functools.partial(kernel, (n_mesh, n_param, levels, pieces)),
            out_shape=jax.ShapeDtypeStruct((rows, modes // n_param), BF16),
            in_specs=[anywhere, anywhere, vmem, vmem],
            out_specs=vmem,
            scratch_shapes=scratch,
            compiler_params=pltpu.CompilerParams(
                collective_id=0, has_side_effects=True, vmem_limit_bytes=48 * 1024 * 1024
            ),
        )(snapshots, coupling, reaction_rate.reshape(1, modes), sketch)

    return jax.shard_map(
        on_device,
        mesh=mesh,
        in_specs=(P("mesh", "param"), P("mesh", None, None, None), P("param"), P()),
        out_specs=P("mesh", "param"),
        check_vma=False,
    )
```

time: 398 us -> 77.7 us (0.20); the launches traced: 392 us -> 77.3 us
  waiting for transfers between devices: 231 us -> 0 us
  other arithmetic: 78.5 us -> 0 us
  Pallas kernels: 0 us -> 71.6 us
  starting transfers between devices: 31.3 us -> 0 us
  matrix products: 25.5 us -> 0 us
  between operations: 13.7 us -> 0.01 us
  local copies, waits for them, and re-layouts: 11.8 us -> 5.63 us
    psum x3 -> x0, waiting for transfers between devices: 193 us -> none  [the longest x2 124 us: on_device(): gram_matrix = lax.psum(column_gram(merged, True), 'mesh')]
    pallas_call x0 -> x1, Pallas kernels: none -> 71.6 us  [on_device(): pl.pallas_call(functools.partial(kernel, (n_mesh, n_param, levels, pieces...]
    another operation x15 -> x0, other arithmetic: 68.7 us -> none  [the longest x9 37.2 us: scaled_inverse(): cholesky_lower = jnp.linalg.cholesky(gram_matrix)]
    ppermute x8 -> x0, waiting for transfers between devices: 38.4 us -> none  [the longest x2 24.9 us: from_partner(): lax.ppermute(shard, axis, [(i, i ^ 1 << stride) for i in range(lax.axis_s...]
    dot_general x11 -> x0, matrix products: 24.7 us -> none  [the longest x2 8.17 us: column_gram(): lax.dot_general(matrix, matrix, (((0,), (0,)), ((), ())), precision=lax.P...]
    ppermute x8 -> x0, starting transfers between devices: 18.1 us -> none  [the longest x3 12.7 us: extended_2(): lax.ppermute(tail, axis, [(i, (i + 1) % count) for i in range(ends)])]
    psum x3 -> x0, starting transfers between devices: 13.2 us -> none  [the longest x2 13.2 us: on_device(): gram_matrix = lax.psum(column_gram(merged, True), 'mesh')]
  transfers between devices with their start and end apart: 11 -> 0, of which waited for: 11 -> 0; matrix products, arithmetic and copies ran while one was open for 0% -> 0% of each run, Pallas kernels for 0% -> 0%
where the time goes in v1:
time: 77.7 us; the launch traced here: 77.3 us
  Pallas kernels  71.6 us (92%)
  local copies, waits for them, and re-layouts  5.63 us (7%)
    pallas_call x1, Pallas kernels, on_device(): pl.pallas_call(functools.partial(kernel, (n_mesh, n_param, levels, pieces...  71.6 us
    unnamed x8, local copies, waits for them, and re-layouts  4.61 us

profile of v1, /device:TPU:0, one launch (start us, length us, event | category | flops | bytes accessed | tf_op | source)
XLA Modules:
  0.0 77.3 jit_solution(17966249967687577670)
XLA Ops:
  0.0 0.0 copy-start
  0.0 1.9 %copy-done = bf16[32,3,128,128]{3,2,1,0:T(8,128)(2,1)S(1)} copy-done((bf16[32,3,128,128]{3,2,1,0:T(8,128)(2,1)S(1)}, bf16[32,3,128,128]{3,2,1,0:T(8,128)(2,1)}, u32[]{:S(2)}) %copy-start) | copy-done | bytes 3145752
  1.9 0.0 copy-start.1
  1.9 1.2 %copy-done.1 = bf16[4096,128]{1,0:T(8,128)(2,1)S(1)} copy-done((bf16[4096,128]{1,0:T(8,128)(2,1)S(1)}, bf16[4096,128]{1,0:T(8,128)(2,1)}, u32[]{:S(2)}) %copy-start.1) | copy-done | bytes 1048600
  3.1 0.0 copy-start.2
  3.1 0.8 %copy-done.2 = bf16[256,128]{1,0:T(8,128)(2,1)S(1)} copy-done((bf16[256,128]{1,0:T(8,128)(2,1)S(1)}, bf16[256,128]{1,0:T(8,128)(2,1)}, u32[]{:S(2)}) %copy-start.2) | copy-done | bytes 65560
  4.0 0.0 copy-start.3
  4.0 0.7 copy-done.3
  4.6 71.6 %shard_map.46 = bf16[4096,32]{1,0:T(8,128)(2,1)S(1)} custom-call(bf16[4096,128]{1,0:T(8,128)(2,1)S(1)} %copy-done.1, bf16[32,3,128,128]{3,2,1,0:T(8,128)(2,1)S(1)} %copy-done, f32[1,128]{1,0:T(1,128)S(1)} %bitcast.1, bf16[256,128]{1,0:T(8,128)(2,1)S(1)} %copy-done.2), custom_call_target="tpu_custom_call" | custom-call | tf_op jit(solution)/shard_map/pallas_call | solution.py:342
  76.2 1.0 %copy.5 = bf16[4096,32]{0,1:T(8,128)(2,1)} copy(bf16[4096,32]{1,0:T(8,128)(2,1)S(1)} %shard_map.46) | data formatting | bytes 524288 | tf_op jit(solution)/shard_map/pallas_call | solution.py:342
Async XLA Ops:
  0.0 1.9 %copy-start = (bf16[32,3,128,128]{3,2,1,0:T(8,128)(2,1)S(1)}, bf16[32,3,128,128]{3,2,1,0:T(8,128)(2,1)}, u32[]{:S(2)}) copy-start(bf16[32,3,128,128]{3,2,1,0:T(8,128)(2,1)} %coup_ref.1) | copy-start | bytes 9437188
  1.9 1.2 %copy-start.1 = (bf16[4096,128]{1,0:T(8,128)(2,1)S(1)}, bf16[4096,128]{1,0:T(8,128)(2,1)}, u32[]{:S(2)}) copy-start(bf16[4096,128]{1,0:T(8,128)(2,1)} %snap_ref.1) | copy-start | bytes 3145732
  3.1 0.8 %copy-start.2 = (bf16[256,128]{1,0:T(8,128)(2,1)S(1)}, bf16[256,128]{1,0:T(8,128)(2,1)}, u32[]{:S(2)}) copy-start(bf16[256,128]{1,0:T(8,128)(2,1)} %sketch_ref.1) | copy-start | bytes 196612
  4.0 0.7 copy-start.3

commit v2 on v1

v2 whole, which is shorter than its diff:
```python
import functools

import jax
import jax.numpy as jnp
from jax import lax
from jax.experimental import pallas as pl
from jax.experimental.pallas import tpu as pltpu
from jax.sharding import PartitionSpec as P

SECTIONS = 3
MESH = pl.DeviceIdType.MESH
F32 = jnp.float32
BF16 = jnp.bfloat16


def split_two(x):
    high = x.astype(BF16)
    return high, (x - high.astype(F32)).astype(BF16)


def reciprocal(x):
    guess = pl.reciprocal(x, approx=True)
    guess = guess * (2.0 - x * guess)
    return guess * (2.0 - x * guess)


def unit_inverse(gram):
    size = gram.shape[0]
    count = size // 8
    tile = (8, size)
    rows = [gram[8 * q : 8 * q + 8, :] for q in range(count)]
    lane = lax.broadcasted_iota(jnp.int32, tile, 1)
    sub = lax.broadcasted_iota(jnp.int32, tile, 0)

    def stacked(parts):
        whole = parts[7]
        for i in range(7):
            whole = jnp.where(sub == i, parts[i], whole)
        return whole

    for p in range(count):
        first = 8 * p
        inside = (lane >= first) & (lane < first + 8)
        corner = [jnp.broadcast_to(rows[p][:, first + j : first + j + 1], tile) for j in range(8)]
        entry = [[jnp.broadcast_to(corner[j][i : i + 1, :], tile) if j >= i else None for j in range(8)] for i in range(8)]
        start = jnp.where(inside, jnp.where(lane - first == sub, 1.0, 0.0), rows[p])
        line = [jnp.broadcast_to(start[i : i + 1, :], tile) for i in range(8)]
        later = [None] * (p + 1) + [jnp.where(inside, 0.0, rows[q]) for q in range(p + 1, count)]
        if p + 1 < count:
            column = [jnp.broadcast_to(rows[p + 1][:, first + j : first + j + 1], tile) for j in range(8)]
        inverse = []
        for i in range(8):
            inverse.append(reciprocal(entry[i][i]))
            for r in range(i + 1, 8):
                scale = entry[i][r] * inverse[i]
                for j in range(r, 8):
                    entry[r][j] = entry[r][j] - scale * entry[i][j]
                line[r] = line[r] - scale * line[i]
            if p + 1 < count:
                scale = column[i] * inverse[i]
                for j in range(i + 1, 8):
                    column[j] = column[j] - scale * entry[i][j]
                later[p + 1] = later[p + 1] - scale * line[i]
        if p + 2 < count:
            turned = stacked([line[i] * inverse[i] for i in range(8)]).T
            for q in range(p + 2, count):
                scales = turned[8 * q : 8 * q + 8, :]
                for i in range(8):
                    later[q] = later[q] - jnp.broadcast_to(scales[:, i : i + 1], tile) * line[i]
        rows[p] = stacked(line)
        rows[p + 1 :] = later[p + 1 :]
    full = jnp.concatenate(rows, 0)
    row = lax.broadcasted_iota(jnp.int32, (size, size), 0)
    column = lax.broadcasted_iota(jnp.int32, (size, size), 1)
    return jnp.where(column <= row, full, 0.0)


def cross(a, b):
    return lax.dot_general(a, b, (((0,), (0,)), ((), ())), preferred_element_type=F32)


def dot(a, b):
    return jnp.dot(a, b, preferred_element_type=F32)


def dot_turned(a, b):
    return lax.dot_general(a, b, (((1,), (1,)), ((), ())), preferred_element_type=F32)


def wait_bytes(ref, sem):
    pltpu.make_async_copy(ref, ref, sem).wait()


def kernel(plan, snap_ref, coup_ref, rate_hbm, sketch_hbm, out_ref, *scratch):
    n_mesh, n_param, levels, pieces = plan
    scratch = list(scratch)
    take = lambda k: [scratch.pop(0) for _ in range(k)]
    coup, rate_ref, sketch_ref, turned, result = take(5)
    states = take(SECTIONS + 1)
    partner_rows = take(levels)
    factors = take(levels)
    partner_factors = take(levels)
    halves = take(levels)
    partial = take(levels + 1)
    slots = take(levels + 1)
    grams = take(levels + 1)
    load_sem, halo_send, halo_recv, merge_send, merge_recv, factor_send, factor_recv, sum_send, sum_recv, all_send, all_recv, out_send, out_recv = take(13)

    m = lax.axis_index("mesh")
    p = lax.axis_index("param")
    total_rows, modes = snap_ref.shape
    block_count, _, block, _ = coup_ref.shape

    load_state = pltpu.make_async_copy(snap_ref, states[0].at[pl.ds(block, total_rows)], load_sem.at[0])
    load_coup = pltpu.make_async_copy(coup_ref, coup, load_sem.at[1])
    load_rate = pltpu.make_async_copy(rate_hbm, rate_ref, load_sem.at[2])
    load_sketch = pltpu.make_async_copy(sketch_hbm, sketch_ref, load_sem.at[3])
    load_state.start()
    load_coup.start()
    load_rate.start()
    load_sketch.start()

    n_all = n_mesh * n_param
    me = m * n_param + p
    barrier = pltpu.get_barrier_semaphore()

    def greet(s, carry):
        t = lax.rem(me + s, n_all)
        pl.semaphore_signal(barrier, inc=1, device_id=(t // n_param, lax.rem(t, n_param)), device_id_type=MESH)
        return carry

    lax.fori_loop(1, n_all, greet, 0)
    for k in range(SECTIONS):
        @pl.when(m == 0)
        def _():
            states[k][pl.ds(0, block), :] = jnp.zeros((block, modes), BF16)

        @pl.when(m == n_mesh - 1)
        def _():
            states[k][pl.ds(block + total_rows, block), :] = jnp.zeros((block, modes), BF16)
    load_state.wait()
    pl.semaphore_wait(barrier, n_all - 1)

    def halo_up(k):
        return pltpu.make_async_remote_copy(
            states[k].at[pl.ds(total_rows, block)], states[k].at[pl.ds(0, block)],
            halo_send.at[2 * k], halo_recv.at[2 * k], device_id=(m + 1, p), device_id_type=MESH)

    def halo_down(k):
        return pltpu.make_async_remote_copy(
            states[k].at[pl.ds(block, block)], states[k].at[pl.ds(block + total_rows, block)],
            halo_send.at[2 * k + 1], halo_recv.at[2 * k + 1], device_id=(m - 1, p), device_id_type=MESH)

    def halo_start(k):
        @pl.when(m < n_mesh - 1)
        def _():
            halo_up(k).start()

        @pl.when(m > 0)
        def _():
            halo_down(k).start()

    halo_start(0)
    load_rate.wait()
    load_sketch.wait()
    load_coup.wait()
    rate = rate_ref[...]

    def advance(k, b):
        c = coup.at[b]
        operator = jnp.concatenate([c[1], c[0], c[2]], 1)
        start = pl.multiple_of(b * block, block)
        mixed = dot(operator, states[k][pl.ds(start, 3 * block), :])
        at = pl.ds(pl.multiple_of(start + block, block), block)
        current = states[k][at, :].astype(F32)
        states[k + 1][at, :] = ((0.5 * current + 0.5 * mixed) / (1.0 + rate * current * current)).astype(BF16)

    inner = block_count - 2
    group = max(g for g in range(1, 11) if inner % g == 0)
    for k in range(SECTIONS):
        def some(i, carry, k=k):
            for j in range(group):
                advance(k, 1 + i * group + j)
            return carry

        lax.fori_loop(0, inner // group, some, 0)

        @pl.when(m > 0)
        def _():
            halo_up(k).wait_recv()

        @pl.when(m < n_mesh - 1)
        def _():
            halo_down(k).wait_recv()

        advance(k, 0)
        advance(k, block_count - 1)
        if k + 1 < SECTIONS:
            halo_start(k + 1)
    state = states[SECTIONS]

    def sum_over(level):
        width = 2**level
        n = n_mesh * width
        count = min(n, pieces)
        depth = modes // count
        base = p // width * width
        rank = m * width + (p - base)

        def device(t):
            return (t // width, base + lax.rem(t, width))

        def scatter(s, carry):
            t = lax.rem(rank + s, n)
            at = pl.ds(pl.multiple_of(lax.rem(t, count) * depth, depth), depth)
            pltpu.make_async_remote_copy(
                partial[level].at[at], slots[level].at[s - 1], sum_send.at[level], sum_recv.at[level],
                device_id=device(t), device_id_type=MESH).start()
            return carry

        lax.fori_loop(1, n, scatter, 0)
        piece = lax.rem(rank, count)
        own = pl.ds(pl.multiple_of(piece * depth, depth), depth)
        wait_bytes(slots[level], sum_recv.at[level])
        if n <= 64:
            total = partial[level][own, :] + jnp.sum(slots[level][...], 0)
        else:
            total = partial[level][own, :] + lax.fori_loop(
                0, n - 1, lambda i, a: a + slots[level][i], jnp.zeros((depth, modes), F32))
        grams[level][own, :] = total

        def spread(s, carry):
            t = rank - piece + lax.rem(piece + s, count)
            pltpu.make_async_remote_copy(
                grams[level].at[own], grams[level].at[own], all_send.at[level], all_recv.at[level],
                device_id=device(t), device_id_type=MESH).start()
            return carry

        lax.fori_loop(1, count, spread, 0)
        wait_bytes(grams[level].at[pl.ds(0, (count - 1) * depth)], all_recv.at[level])
        return grams[level][...]

    chunk = 512

    def merge_copy(level):
        half = total_rows // 2 ** (level + 1)
        keep = p // 2**level % 2
        if level == 0:
            source = state.at[pl.ds(pl.multiple_of(block + (1 - keep) * half, 16), half)]
        else:
            source = halves[level - 1].at[pl.ds(pl.multiple_of((1 - keep) * half, 16), half)]
        return pltpu.make_async_remote_copy(
            source, partner_rows[level], merge_send.at[level], merge_recv.at[level],
            device_id=(m, p + (1 - 2 * keep) * 2**level), device_id_type=MESH)

    def factor_copy(level):
        keep = p // 2**level % 2
        return pltpu.make_async_remote_copy(
            factors[level], partner_factors[level], factor_send.at[level], factor_recv.at[level],
            device_id=(m, p + (1 - 2 * keep) * 2**level), device_id_type=MESH)

    merge_copy(0).start()
    gram = jnp.zeros((modes, modes), F32)
    for i in range(total_rows // chunk):
        part = state[pl.ds(block + i * chunk, chunk), :]
        gram += cross(part, part)
    partial[0][...] = gram
    factors[0][...] = unit_inverse(sum_over(0)).astype(BF16)

    for level in range(levels):
        half = total_rows // 2 ** (level + 1)
        keep = p // 2**level % 2
        step = min(half, chunk)
        steps = range(half // step)
        factor_copy(level).start()
        mine = sketch_ref[pl.ds(pl.multiple_of(keep * modes, modes), modes), :]
        theirs = sketch_ref[pl.ds(pl.multiple_of((1 - keep) * modes, modes), modes), :]
        weights = jnp.concatenate([mine, theirs], 0)

        def basis_of(pair, factor):
            if level == 0:
                return dot_turned(pair, factor).astype(BF16)
            high = factor[:, :modes]
            total = dot_turned(pair, jnp.concatenate([high, high], 1)) + dot_turned(pair[:, :modes], factor[:, modes:])
            return total.astype(BF16)

        factor = factors[level][...]
        kept = []
        for i in steps:
            at = keep * half + i * step
            if level == 0:
                pair = state[pl.ds(pl.multiple_of(at + block, 16), step), :]
            else:
                pair = halves[level - 1][pl.ds(pl.multiple_of(at, 16), step), :]
            kept.append(basis_of(pair, factor))
        merge_copy(level).wait_recv()
        factor_copy(level).wait_recv()
        factor = partner_factors[level][...]
        gram = jnp.zeros((modes, 2 * modes), F32)
        for i in steps:
            other = basis_of(partner_rows[level][pl.ds(i * step, step), :], factor)
            high, low = split_two(dot(jnp.concatenate([kept[i], other], 1), weights))
            pair = jnp.concatenate([high, low], 1)
            halves[level][pl.ds(i * step, step), :] = pair
            gram += cross(high, pair)
        if level + 1 < levels:
            merge_copy(level + 1).start()
        partial[level + 1][...] = gram[:, :modes] + gram[:, modes:] + gram[:, modes:].T
        high, low = split_two(unit_inverse(sum_over(level + 1)))
        if level + 1 < levels:
            factors[level + 1][...] = jnp.concatenate([high, low], 1)

    share = modes // n_param
    rows = total_rows // n_param
    step = min(rows, chunk)
    twice = jnp.concatenate([high, high], 1)
    for i in range(rows // step):
        pair = halves[levels - 1][pl.ds(i * step, step), :]
        turned[:, pl.ds(i * step, step)] = (dot_turned(twice, pair) + dot_turned(low, pair[:, :modes])).astype(BF16)
    offset = 0
    for level in range(levels):
        offset = offset + p // 2**level % 2 * (total_rows // 2 ** (level + 1))
    place = pl.ds(pl.multiple_of(offset, 128), rows)

    def deliver(s, carry):
        t = lax.rem(p + s, n_param)
        pltpu.make_async_remote_copy(
            turned.at[pl.ds(pl.multiple_of(t * share, 16), share)], result.at[:, place], out_send.at[0], out_recv.at[0],
            device_id=(m, t), device_id_type=MESH).start()
        return carry

    lax.fori_loop(1, n_param, deliver, 0)
    result[:, place] = turned[pl.ds(pl.multiple_of(p * share, 16), share), :]
    others = result.at[:, pl.ds(0, (n_param - 1) * rows)]
    wait_bytes(others, out_recv.at[0])
    out_ref[...] = result[...]

    for k in range(SECTIONS):
        @pl.when(m < n_mesh - 1)
        def _():
            halo_up(k).wait_send()

        @pl.when(m > 0)
        def _():
            halo_down(k).wait_send()
    for level in range(levels):
        merge_copy(level).wait_send()
        factor_copy(level).wait_send()
    for level in range(levels + 1):
        count = min(n_mesh * 2**level, pieces)
        wait_bytes(slots[level], sum_send.at[level])
        wait_bytes(grams[level].at[pl.ds(0, (count - 1) * (modes // count))], all_send.at[level])
    wait_bytes(others, out_send.at[0])


def solution(mesh):
    n_mesh, n_param = mesh.shape["mesh"], mesh.shape["param"]
    levels = n_param.bit_length() - 1

    def on_device(snapshots, coupling, reaction_rate, sketch):
        rows, modes = snapshots.shape
        block = coupling.shape[2]
        pieces = modes // 8
        square = pltpu.VMEM((modes, modes), F32)
        slots = []
        for level in range(levels + 1):
            n = n_mesh * 2**level
            slots.append(pltpu.VMEM((n - 1, modes // min(n, pieces), modes), F32))
        dma = lambda k: pltpu.SemaphoreType.DMA((k,))
        share = modes // n_param
        widths = [modes] + [2 * modes] * (levels - 1)
        scratch = [
            pltpu.VMEM(coupling.shape, BF16),
            pltpu.VMEM((1, modes), F32),
            pltpu.VMEM(sketch.shape, BF16),
            pltpu.VMEM((modes, rows // n_param), BF16),
            pltpu.VMEM((share, rows), BF16),
        ]
        scratch += [pltpu.VMEM((rows + 2 * block, modes), BF16)] * (SECTIONS + 1)
        scratch += [pltpu.VMEM((rows >> (k + 1), widths[k]), BF16) for k in range(levels)]
        scratch += [pltpu.VMEM((modes, widths[k]), BF16) for k in range(levels)] * 2
        scratch += [pltpu.VMEM((rows >> (k + 1), 2 * modes), BF16) for k in range(levels)]
        scratch += [square] * (levels + 1) + slots + [square] * (levels + 1)
        scratch += [dma(4), dma(2 * SECTIONS), dma(2 * SECTIONS)] + [dma(levels)] * 4
        scratch += [dma(levels + 1)] * 4 + [dma(1), dma(1)]
        vmem = pl.BlockSpec(memory_space=pltpu.VMEM)
        anywhere = pl.BlockSpec(memory_space=pltpu.HBM)
        return pl.pallas_call(
            functools.partial(kernel, (n_mesh, n_param, levels, pieces)),
            out_shape=jax.ShapeDtypeStruct((share, rows), BF16),
            in_specs=[anywhere] * 4,
            out_specs=vmem,
            scratch_shapes=scratch,
            compiler_params=pltpu.CompilerParams(
                collective_id=0, has_side_effects=True, vmem_limit_bytes=63 * 1024 * 1024
            ),
        )(snapshots, coupling, reaction_rate.reshape(1, modes), sketch).T

    return jax.shard_map(
        on_device,
        mesh=mesh,
        in_specs=(P("mesh", "param"), P("mesh", None, None, None), P("param"), P()),
        out_specs=P("mesh", "param"),
        check_vma=False,
    )
```

time: 77.7 us -> 73.1 us (0.941)
  local copies, waits for them, and re-layouts: 5.63 us -> 1.67 us
    unnamed x8 -> x1, local copies, waits for them, and re-layouts: 4.61 us -> 1.67 us
    pallas_call x1 -> x0, local copies, waits for them, and re-layouts: 1.03 us -> none  [on_device(): pl.pallas_call(functools.partial(kernel, (n_mesh, n_param, levels, pieces...]
where the time goes in v2:
time: 73.1 us; the launch traced here: 72.7 us
  Pallas kernels  71 us (97%)
  local copies, waits for them, and re-layouts  1.67 us (2%)
    pallas_call x1, Pallas kernels, on_device(): pl.pallas_call(functools.partial(kernel, (n_mesh, n_param, levels, pieces...  71 us
    unnamed x1, local copies, waits for them, and re-layouts  1.67 us

profile of v2, /device:TPU:0, one launch (start us, length us, event | category | flops | bytes accessed | tf_op | source)
XLA Modules:
  0.0 72.7 jit_solution(7429995641120853871)
XLA Ops:
  0.0 71.0 %shard_map.46 = bf16[32,4096]{1,0:T(8,128)(2,1)} custom-call(bf16[4096,128]{1,0:T(8,128)(2,1)} %snap_ref.1, bf16[32,3,128,128]{3,2,1,0:T(8,128)(2,1)} %coup_ref.1, f32[1,128]{1,0:T(1,128)} %bitcast.3, bf16[256,128]{1,0:T(8,128)(2,1)} %sketch_hbm.1), custom_call_target="tpu_custom_call" | custom-call | tf_op jit(solution)/shard_map/pallas_call | solution.py:388
  71.0 1.7 %copy.6 = bf16[4096,32]{0,1:T(8,128)(2,1)} copy(bf16[4096,32]{0,1:T(8,128)(2,1)} %bitcast.2) | data formatting | bytes 524288

commit v3 on v2

--- a/solution.py
+++ b/solution.py
@@ -18,9 +18,14 @@
     return high, (x - high.astype(F32)).astype(BF16)
 
 
+def split_three(x):
+    high = x.astype(BF16).astype(F32)
+    middle = (x - high).astype(BF16).astype(F32)
+    return high, middle, x - high - middle
+
+
 def reciprocal(x):
     guess = pl.reciprocal(x, approx=True)
-    guess = guess * (2.0 - x * guess)
     return guess * (2.0 - x * guess)
 
 
@@ -62,11 +67,14 @@
                     column[j] = column[j] - scale * entry[i][j]
                 later[p + 1] = later[p + 1] - scale * line[i]
         if p + 2 < count:
-            turned = stacked([line[i] * inverse[i] for i in range(8)]).T
+            left = split_three(stacked([line[i] * inverse[i] for i in range(8)]))
+            right = split_three(stacked(line))
+            terms = ((0, 0), (0, 1), (1, 0), (0, 2), (2, 0), (1, 1))
+            change = cross(
+                jnp.concatenate([left[i] for i, _ in terms], 0).astype(BF16),
+                jnp.concatenate([right[j] for _, j in terms], 0).astype(BF16))
             for q in range(p + 2, count):
-                scales = turned[8 * q : 8 * q + 8, :]
-                for i in range(8):
-                    later[q] = later[q] - jnp.broadcast_to(scales[:, i : i + 1], tile) * line[i]
+                later[q] = later[q] - change[8 * q : 8 * q + 8, :]
         rows[p] = stacked(line)
         rows[p + 1 :] = later[p + 1 :]
     full = jnp.concatenate(rows, 0)
@@ -173,7 +181,7 @@
         mixed = dot(operator, states[k][pl.ds(start, 3 * block), :])
         at = pl.ds(pl.multiple_of(start + block, block), block)
         current = states[k][at, :].astype(F32)
-        states[k + 1][at, :] = ((0.5 * current + 0.5 * mixed) / (1.0 + rate * current * current)).astype(BF16)
+        states[k + 1][at, :] = ((0.5 * current + 0.5 * mixed) * reciprocal(1.0 + rate * current * current)).astype(BF16)
 
     inner = block_count - 2
     group = max(g for g in range(1, 11) if inner % g == 0)

time: 73.1 us -> 68.9 us (0.943)
  Pallas kernels: 71 us -> 66.9 us
    pallas_call x1, Pallas kernels: 71 us -> 66.9 us  [on_device(): pl.pallas_call(functools.partial(kernel, (n_mesh, n_param, levels, pieces...]
where the time goes in v3:
time: 68.9 us; the launch traced here: 68.5 us
  Pallas kernels  66.9 us (97%)
  local copies, waits for them, and re-layouts  1.67 us (2%)
    pallas_call x1, Pallas kernels, on_device(): pl.pallas_call(functools.partial(kernel, (n_mesh, n_param, levels, pieces...  66.9 us
    unnamed x1, local copies, waits for them, and re-layouts  1.67 us

profile of v3, /device:TPU:0, one launch (start us, length us, event | category | flops | bytes accessed | tf_op | source)
XLA Modules:
  0.0 68.5 jit_solution(3264512526253991602)
XLA Ops:
  0.0 66.9 %shard_map.46 = bf16[32,4096]{1,0:T(8,128)(2,1)} custom-call(bf16[4096,128]{1,0:T(8,128)(2,1)} %snap_ref.1, bf16[32,3,128,128]{3,2,1,0:T(8,128)(2,1)} %coup_ref.1, f32[1,128]{1,0:T(1,128)} %bitcast.3, bf16[256,128]{1,0:T(8,128)(2,1)} %sketch_hbm.1), custom_call_target="tpu_custom_call" | custom-call | tf_op jit(solution)/shard_map/pallas_call | solution.py:396
  66.9 1.7 %copy.6 = bf16[4096,32]{0,1:T(8,128)(2,1)} copy(bf16[4096,32]{0,1:T(8,128)(2,1)} %bitcast.2) | data formatting | bytes 524288
